TPU v7x, 32 devices: a whole 2x2x4 slice. The times are simulated.
32 devices in a mesh: seq: 8 (over z, x), head: 4 (over y, core).
Axes of the slice: x: 2, y: 2, z: 4, core: 2. Of those that a mesh axis runs over, the one named last changes fastest.
Arguments:
- query: bfloat16 [4, 4096, 128], P('head', 'seq'), may hold values from -8 to 8
- key: bfloat16 [4, 4096, 128], P('head', 'seq'), may hold values from -8 to 8
- value: bfloat16 [4, 4096, 128], P('head', 'seq'), may hold values from -16 to 16
- lin_query: bfloat16 [4, 4096, 128], P('head', 'seq'), may hold values from -52 to 52
- lin_key: bfloat16 [4, 4096, 128], P('head', 'seq'), may hold values from -5 to 5
- gain: float32 [4, 128], P('head'), may hold values from 0.25 to 1.75
- cotangent: bfloat16 [4, 4096, 128], P('head', 'seq'), may hold values from -16 to 16
- key_block: int32 [32, 20], replicated, may hold values from -1 to 31, as said below
Outputs:
- mixed: bfloat16 [4, 4096, 128], P('head', 'seq')
- grad_query: bfloat16 [4, 4096, 128], P('head', 'seq')
- grad_key: bfloat16 [4, 4096, 128], P('head', 'seq')
- grad_value: bfloat16 [4, 4096, 128], P('head', 'seq')
- grad_lin_query: bfloat16 [4, 4096, 128], P('head', 'seq')
- grad_lin_key: bfloat16 [4, 4096, 128], P('head', 'seq')
- grad_gain: float32 [4, 128], P('head')
Inputs may be any that keep to these rules, and one draw needn't show every extreme that they name: `key_block`: row b lists the key blocks that query block b reads: slot 0 is b, slot 1 is b - 1 (-1 when b is 0); each later slot names a block that lies on an earlier index of seq than b and before b - 1, or is -1, and all -1 slots follow the named ones. A row names no block twice. Over all rows' slots from 2 on, at most one block of the blocks on one index of seq is named.
All inputs are finite; a program needn't handle non-finite values.
Results may differ from a plain program's by a relative error of at most 0.039.
Values may be sent and summed in bfloat16 or wider, within the bound.
A program may use at most 64 MiB of HBM per device.

v0:
```python
import jax
import jax.numpy as jnp
from jax import lax
from jax.sharding import PartitionSpec as P

BLK = 128


masked_value = -1e30
eps_norm = 1e-05


def passed_along(value, axis, by):
    size = lax.axis_size(axis)
    pairs = [(i, i + by) for i in range(size) if 0 <= i + by < size]
    return lax.ppermute(value, axis, pairs)


def pool_slots(names, base, per_dev):
    slot = jnp.arange(names.shape[1])[None, :]
    live = names >= 0
    own = names - base
    local = jnp.where(own >= 0, own, per_dev)
    remote = per_dev + 1 + names // per_dev
    place = jnp.where(slot == 0, own, jnp.where(slot == 1, local, remote))
    return (jnp.where(live, place, 0), live)


def allowed_mask(live, blk):
    causal = jnp.arange(blk)[:, None] >= jnp.arange(blk)[None, :]
    first = jnp.arange(live.shape[1]) == 0
    return live[:, None, :, None] & (
        jnp.logical_not(first)[None, None, :, None] | causal[None, :, None, :]
    )


def earlier_sum(local):

    def earlier_relay(step, carry):
        return passed_along(carry + local, "seq", 1)

    return lax.fori_loop(0, lax.axis_size("seq") - 1, earlier_relay, jnp.zeros_like(local))


def later_sum(local):

    def later_relay(step, carry):
        return passed_along(carry + local, "seq", -1)

    return lax.fori_loop(0, lax.axis_size("seq") - 1, later_relay, jnp.zeros_like(local))


def far_gradients(terms_key, terms_value):
    parts_key, parts_value = (
        lax.all_to_all(
            terms_key.astype(jnp.bfloat16), "seq", split_axis=1, concat_axis=1, tiled=True
        ).astype(terms_key.dtype),
        lax.all_to_all(
            terms_value.astype(jnp.bfloat16), "seq", split_axis=1, concat_axis=1, tiled=True
        ).astype(terms_value.dtype),
    )
    return (jnp.sum(parts_key, axis=1, keepdims=True), jnp.sum(parts_value, axis=1, keepdims=True))


def group_scores(rows_q, keys_g, allow, scale):
    scores = (
        jnp.einsum("hgqd,hgjkd->hgqjk", rows_q, keys_g, preferred_element_type=jnp.float32) * scale
    )
    return jnp.where(allow[None], scores, masked_value)


def per_device(query, key, value, lin_query, lin_key, gain, cotangent, key_block):
    f32 = jnp.float32
    bf16 = jnp.bfloat16
    hi = lax.Precision.HIGHEST
    heads, rows, width = query.shape
    blk = BLK
    per_dev = rows // blk
    ndev = lax.axis_size("seq")
    me = lax.axis_index("seq")
    base = me * per_dev
    nblk = key_block.shape[0]
    scale = width ** (-0.5)
    features = heads * lax.axis_size("head") * width
    far_names = key_block[:, 2:]
    used = (
        jnp.zeros((nblk,), jnp.int32)
        .at[jnp.maximum(far_names, 0).reshape(-1)]
        .max((far_names >= 0).astype(jnp.int32).reshape(-1))
    )
    chosen = jnp.sum(
        used.reshape(ndev, per_dev) * jnp.arange(per_dev, dtype=jnp.int32)[None, :], axis=1
    )
    mine = chosen[me]
    key_blocks = key.reshape(heads, per_dev, blk, width)
    value_blocks = value.reshape(heads, per_dev, blk, width)
    query_blocks = query.reshape(heads, per_dev, blk, width)
    own_key = lax.dynamic_index_in_dim(key_blocks, mine, 1, keepdims=True)
    own_value = lax.dynamic_index_in_dim(value_blocks, mine, 1, keepdims=True)
    far_key, far_value = (
        lax.all_gather(own_key, "seq", axis=1, tiled=True),
        lax.all_gather(own_value, "seq", axis=1, tiled=True),
    )
    prev_key, prev_value = passed_along(
        (key_blocks[:, per_dev - 1 :], value_blocks[:, per_dev - 1 :]), "seq", 1
    )
    pool_key = jnp.concatenate([key_blocks, prev_key, far_key], axis=1)
    pool_value = jnp.concatenate([value_blocks, prev_value, far_value], axis=1)
    names = lax.dynamic_slice_in_dim(key_block, base, per_dev, 0)
    slots, live = pool_slots(names, base, per_dev)
    allow = allowed_mask(live, blk)
    keys_g = pool_key[:, slots]
    values_g = pool_value[:, slots]
    scores = group_scores(query_blocks, keys_g, allow, scale)
    row_max = jnp.max(scores, axis=(3, 4), keepdims=True)
    weights = jnp.exp(scores - row_max)
    total = jnp.sum(weights, axis=(3, 4), keepdims=True)
    summed = jnp.einsum(
        "hgqjk,hgjkd->hgqd", weights.astype(bf16), values_g, preferred_element_type=f32
    )
    attended_parts = (summed / total[..., 0]).astype(bf16)
    log_parts = (row_max + jnp.log(total))[..., 0, 0]
    att_f = attended_parts.astype(f32)
    lq_b = lin_query.reshape(heads, per_dev, blk, width)
    lk_b = lin_key.reshape(heads, per_dev, blk, width)
    lq = lq_b.astype(f32)
    lk = lk_b.astype(f32)
    lower = (jnp.arange(blk)[:, None] >= jnp.arange(blk)[None, :]).astype(f32)
    block_states = jnp.einsum("hbki,hbkj->hbij", lk_b, attended_parts, preferred_element_type=f32)
    incoming = earlier_sum(jnp.sum(block_states, axis=1))
    prior = incoming[:, None] + jnp.cumsum(block_states, axis=1) - block_states
    mixing = jnp.einsum("hbqi,hbki->hbqk", lq_b, lk_b, preferred_element_type=f32) * lower
    linear = jnp.einsum("hbqk,hbkd->hbqd", mixing, att_f, precision=hi) + jnp.einsum(
        "hbqi,hbij->hbqj", lq, prior, precision=hi
    )
    squares = lax.psum(jnp.sum(linear * linear, axis=(0, 3)), "head")
    inv_rms = lax.rsqrt(squares / features + eps_norm)
    normed = linear * inv_rms[None, :, :, None]
    mixed = (att_f + gain[:, None, None, :] * normed).astype(bf16).reshape(heads, rows, width)
    grad_out = cotangent.reshape(heads, per_dev, blk, width).astype(f32)
    grad_gain = lax.psum(jnp.sum(grad_out * normed, axis=(1, 2)), "seq")
    scaled = grad_out * gain[:, None, None, :]
    inner = lax.psum(jnp.sum(scaled * normed, axis=(0, 3)), "head")
    grad_linear = inv_rms[None, :, :, None] * (
        scaled - normed * (inner / features)[None, :, :, None]
    )
    pairs = jnp.einsum("hbqd,hbkd->hbqk", grad_linear, att_f, precision=hi) * lower
    grad_lq = jnp.einsum("hbqk,hbki->hbqi", pairs, lk, precision=hi) + jnp.einsum(
        "hbqj,hbij->hbqi", grad_linear, prior, precision=hi
    )
    block_grads = jnp.einsum("hbti,hbtj->hbij", lq, grad_linear, precision=hi)
    later = later_sum(jnp.sum(block_grads, axis=1))
    after = (
        later[:, None]
        + jnp.sum(block_grads, axis=1, keepdims=True)
        - jnp.cumsum(block_grads, axis=1)
    )
    grad_lk = jnp.einsum("hbqk,hbqi->hbki", pairs, lq, precision=hi) + jnp.einsum(
        "hbkj,hbij->hbki", att_f, after, precision=hi
    )
    grad_att = (
        grad_out
        + jnp.einsum("hbqk,hbqd->hbkd", mixing, grad_linear, precision=hi)
        + jnp.einsum("hbki,hbij->hbkj", lk, after, precision=hi)
    )
    grad_att_b = grad_att.astype(bf16)
    delta = jnp.sum(grad_att_b.astype(f32) * att_f, axis=3)
    pool_count = pool_key.shape[1]
    grad_pool_key = jnp.zeros((heads, pool_count, blk, width), f32)
    grad_pool_value = jnp.zeros((heads, pool_count, blk, width), f32)
    allow = allowed_mask(live, blk)
    keys_g = pool_key[:, slots]
    values_g = pool_value[:, slots]
    scores = group_scores(query_blocks, keys_g, allow, scale)
    probs = jnp.exp(scores - log_parts[..., None, None])
    grad_probs = jnp.einsum("hgqd,hgjkd->hgqjk", grad_att_b, values_g, preferred_element_type=f32)
    grad_scores = (probs * (grad_probs - delta[..., None, None])).astype(bf16)
    grad_q_parts = (
        jnp.einsum("hgqjk,hgjkd->hgqd", grad_scores, keys_g, preferred_element_type=f32) * scale
    ).astype(bf16)
    part_key = (
        jnp.einsum("hgqjk,hgqd->hgjkd", grad_scores, query_blocks, preferred_element_type=f32)
        * scale
    )
    part_value = jnp.einsum(
        "hgqjk,hgqd->hgjkd", probs.astype(bf16), grad_att_b, preferred_element_type=f32
    )
    grad_pool_key = grad_pool_key.at[:, slots].add(part_key)
    grad_pool_value = grad_pool_value.at[:, slots].add(part_value)
    back_key, back_value = (
        passed_along(
            grad_pool_key[:, per_dev : per_dev + 1].astype(jnp.bfloat16), "seq", -1
        ).astype(jnp.float32),
        passed_along(
            grad_pool_value[:, per_dev : per_dev + 1].astype(jnp.bfloat16), "seq", -1
        ).astype(jnp.float32),
    )
    far_gk, far_gv = far_gradients(
        grad_pool_key[:, per_dev + 1 :], grad_pool_value[:, per_dev + 1 :]
    )
    is_mine = (jnp.arange(per_dev) == mine)[None, :, None, None]
    is_last = (jnp.arange(per_dev) == per_dev - 1)[None, :, None, None]
    own_gk = (
        grad_pool_key[:, :per_dev]
        + jnp.where(is_last, back_key, 0.0)
        + jnp.where(is_mine, far_gk, 0.0)
    )
    own_gv = (
        grad_pool_value[:, :per_dev]
        + jnp.where(is_last, back_value, 0.0)
        + jnp.where(is_mine, far_gv, 0.0)
    )
    grad_query = grad_q_parts.reshape(heads, rows, width)
    grad_key = own_gk.astype(bf16).reshape(heads, rows, width)
    grad_value = own_gv.astype(bf16).reshape(heads, rows, width)
    grad_lin_query = grad_lq.astype(bf16).reshape(heads, rows, width)
    grad_lin_key = grad_lk.astype(bf16).reshape(heads, rows, width)
    return (mixed, grad_query, grad_key, grad_value, grad_lin_query, grad_lin_key, grad_gain)


def solution(mesh):
    in_specs = (
        P("head", "seq", None),
        P("head", "seq", None),
        P("head", "seq", None),
        P("head", "seq", None),
        P("head", "seq", None),
        P("head", None),
        P("head", "seq", None),
        P(),
    )
    out_specs = (
        P("head", "seq", None),
        P("head", "seq", None),
        P("head", "seq", None),
        P("head", "seq", None),
        P("head", "seq", None),
        P("head", "seq", None),
        P("head", None),
    )
    return jax.shard_map(
        per_device, mesh=mesh, in_specs=in_specs, out_specs=out_specs, check_vma=False
    )
```

profile of v0, /device:TPU:0, one launch (start us, length us, event | category | flops | bytes accessed | tf_op | source)
XLA Modules:
  0.0 301.6 jit_solution(16939196685743618146)
XLA Ops:
  2.5 5.6 %scatter_custom_fusion = s32[32]{0:T(128)S(1)} fusion(s32[576]{0:T(1024)S(1)} %fusion.46, s32[576]{0:T(1024)S(1)} %reshape.433, s32[]{:T(128)} %copy.103), kind=kCustom, calls=%fused_computation.99 | custom fusion | flops 576 | bytes 132 | tf_op jit(solution)/shard_map/scatter-max | solution.py:89
  11.6 4.8 %collective-permute-start.3 = (bf16[1,1,128,128]{3,2,0,1:T(8,128)(2,1)S(1)}, bf16[1,1,128,128]{3,2,0,1:T(8,128)(2,1)S(1)}, u32[]{:S(2)}, u32[]{:S(2)}) collective-permute-start(bf16[1,1,128,128]{3,2,0,1:T(8,128)(2,1)S(1)} %get-tuple-element.68), channel_id=1, source_target_pairs={{0,4},{4,8},{8,12},{12,16},{16,20},{20,24},{24,28},{1,5},{5,9},{9,... | collective-permute-start | bytes 98312 | tf_op jit(solution)/shard_map/ppermute | solution.py:16
  21.9 30.8 %all_gather.7 = bf16[1,8,128,128]{3,2,0,1:T(8,128)(2,1)S(1)} all-gather(bf16[1,1,128,128]{3,2,0,1:T(8,128)(2,1)S(1)} %get-tuple-element.69), channel_id=1, replica_groups=mesh['seq'=8,'head'=4] {'seq'}, dimensions={1}, use_global_device_ids=true | all-gather | bytes 294912 | tf_op jit(solution)/shard_map/all_gather | solution.py:102
  53.7 32.7 %all_gather.6 = bf16[1,8,128,128]{3,2,0,1:T(8,128)(2,1)} all-gather(bf16[1,1,128,128]{3,2,0,1:T(8,128)(2,1)S(1)} %get-tuple-element.67), channel_id=1, replica_groups=mesh['seq'=8,'head'=4] {'seq'}, dimensions={1}, use_global_device_ids=true | all-gather | bytes 294912 | tf_op jit(solution)/shard_map/all_gather | solution.py:101
  101.3 43.6 %while.20 = (s32[]{:T(128)}, f32[1,128,128]{2,1,0:T(8,128)S(1)}, f32[1,128,128]{2,1,0:T(8,128)S(1)}, s32[]{:T(128)}) while((s32[]{:T(128)}, f32[1,128,128]{2,1,0:T(8,128)S(1)}, f32[1,128,128]{2,1,0:T(8,128)S(1)}, s32[]{:T(128)}) %tuple.50), condition=%wide.region_6.7_spmd, body=%wide.region_5.6_spmd.sunk | while | flops 16386 | bytes 458845 | solution.py:42
  123.3 5.4 %collective-permute-start = (f32[1,128,128]{2,1,0:T(8,128)S(1)}, f32[1,128,128]{2,1,0:T(8,128)S(1)}, u32[]{:S(2)}, u32[]{:S(2)}) collective-permute-start(f32[1,128,128]{2,1,0:T(8,128)S(1)} %add.214), channel_id=1, source_target_pairs={{0,4},{4,8},{8,12},{12,16},{16,20},{20,24},{24,28},{1,5},{5,9},{9,... | collective-permute-start | bytes 196616 | tf_op jit(solution)/shard_map/while/body/eval_jaxpr/ppermute | solution.py:16
  130.6 5.3 %collective-permute-start = (f32[1,128,128]{2,1,0:T(8,128)S(1)}, f32[1,128,128]{2,1,0:T(8,128)S(1)}, u32[]{:S(2)}, u32[]{:S(2)}) collective-permute-start(f32[1,128,128]{2,1,0:T(8,128)S(1)} %add.214), channel_id=1, source_target_pairs={{0,4},{4,8},{8,12},{12,16},{16,20},{20,24},{24,28},{1,5},{5,9},{9,... | collective-permute-start | bytes 196616 | tf_op jit(solution)/shard_map/while/body/eval_jaxpr/ppermute | solution.py:16
  137.8 5.2 %collective-permute-start = (f32[1,128,128]{2,1,0:T(8,128)S(1)}, f32[1,128,128]{2,1,0:T(8,128)S(1)}, u32[]{:S(2)}, u32[]{:S(2)}) collective-permute-start(f32[1,128,128]{2,1,0:T(8,128)S(1)} %add.214), channel_id=1, source_target_pairs={{0,4},{4,8},{8,12},{12,16},{16,20},{20,24},{24,28},{1,5},{5,9},{9,... | collective-permute-start | bytes 196616 | tf_op jit(solution)/shard_map/while/body/eval_jaxpr/ppermute | solution.py:16
  146.5 5.7 %psum.21 = f32[4,128]{1,0:T(4,128)S(1)} all-reduce(f32[4,128]{1,0:T(4,128)S(1)} %get-tuple-element.76), channel_id=1, replica_groups=mesh['seq'=8,'head'=4] {'head'}, use_global_device_ids=true, to_apply=%region_9.10 | all-reduce | flops 512 | bytes 4096 | tf_op jit(solution)/shard_map/psum | solution.py:136
  153.0 6.8 %psum.22 = f32[4,128]{1,0:T(4,128)S(1)} all-reduce(f32[4,128]{1,0:T(4,128)S(1)} %get-tuple-element.50), channel_id=1, replica_groups=mesh['seq'=8,'head'=4] {'head'}, use_global_device_ids=true, to_apply=%region_11.12 | all-reduce | flops 512 | bytes 4096 | tf_op jit(solution)/shard_map/psum | solution.py:143
  161.3 50.5 %while.21 = (s32[]{:T(128)}, f32[1,128,128]{2,1,0:T(8,128)S(1)}, f32[1,128,128]{2,1,0:T(8,128)S(1)}, s32[]{:T(128)}) while((s32[]{:T(128)}, f32[1,128,128]{2,1,0:T(8,128)S(1)}, f32[1,128,128]{2,1,0:T(8,128)S(1)}, s32[]{:T(128)}) %tuple.53), condition=%wide.region_14.15_spmd, body=%wide.region_13.14_spmd.sunk | while | flops 16386 | bytes 458845 | solution.py:50
  162.6 6.1 %collective-permute-done.1 = f32[1,128,128]{2,1,0:T(8,128)S(1)} collective-permute-done((f32[1,128,128]{2,1,0:T(8,128)S(1)}, f32[1,128,128]{2,1,0:T(8,128)S(1)}, u32[]{:S(2)}, u32[]{:S(2)}) %collective-permute-start.1) | collective-permute-done | bytes 65568 | tf_op jit(solution)/shard_map/while/body/eval_jaxpr/ppermute | solution.py:16
  170.0 6.1 %collective-permute-done.1 = f32[1,128,128]{2,1,0:T(8,128)S(1)} collective-permute-done((f32[1,128,128]{2,1,0:T(8,128)S(1)}, f32[1,128,128]{2,1,0:T(8,128)S(1)}, u32[]{:S(2)}, u32[]{:S(2)}) %collective-permute-start.1) | collective-permute-done | bytes 65568 | tf_op jit(solution)/shard_map/while/body/eval_jaxpr/ppermute | solution.py:16
  177.4 5.8 %collective-permute-done.1 = f32[1,128,128]{2,1,0:T(8,128)S(1)} collective-permute-done((f32[1,128,128]{2,1,0:T(8,128)S(1)}, f32[1,128,128]{2,1,0:T(8,128)S(1)}, u32[]{:S(2)}, u32[]{:S(2)}) %collective-permute-start.1) | collective-permute-done | bytes 65568 | tf_op jit(solution)/shard_map/while/body/eval_jaxpr/ppermute | solution.py:16
  184.5 5.8 %collective-permute-done.1 = f32[1,128,128]{2,1,0:T(8,128)S(1)} collective-permute-done((f32[1,128,128]{2,1,0:T(8,128)S(1)}, f32[1,128,128]{2,1,0:T(8,128)S(1)}, u32[]{:S(2)}, u32[]{:S(2)}) %collective-permute-start.1) | collective-permute-done | bytes 65568 | tf_op jit(solution)/shard_map/while/body/eval_jaxpr/ppermute | solution.py:16
  191.6 6.4 %collective-permute-done.1 = f32[1,128,128]{2,1,0:T(8,128)S(1)} collective-permute-done((f32[1,128,128]{2,1,0:T(8,128)S(1)}, f32[1,128,128]{2,1,0:T(8,128)S(1)}, u32[]{:S(2)}, u32[]{:S(2)}) %collective-permute-start.1) | collective-permute-done | bytes 65568 | tf_op jit(solution)/shard_map/while/body/eval_jaxpr/ppermute | solution.py:16
  199.2 5.5 %collective-permute-done.1 = f32[1,128,128]{2,1,0:T(8,128)S(1)} collective-permute-done((f32[1,128,128]{2,1,0:T(8,128)S(1)}, f32[1,128,128]{2,1,0:T(8,128)S(1)}, u32[]{:S(2)}, u32[]{:S(2)}) %collective-permute-start.1) | collective-permute-done | bytes 65568 | tf_op jit(solution)/shard_map/while/body/eval_jaxpr/ppermute | solution.py:16
  206.0 5.8 %collective-permute-done.1 = f32[1,128,128]{2,1,0:T(8,128)S(1)} collective-permute-done((f32[1,128,128]{2,1,0:T(8,128)S(1)}, f32[1,128,128]{2,1,0:T(8,128)S(1)}, u32[]{:S(2)}, u32[]{:S(2)}) %collective-permute-start.1) | collective-permute-done | bytes 65568 | tf_op jit(solution)/shard_map/while/body/eval_jaxpr/ppermute | solution.py:16
  212.4 5.7 %fusion.3 = f32[4,20,128,128]{3,2,1,0:T(8,128)} fusion(f32[4,128,20,128]{1,3,2,0:T(8,128)} %copy-done.1, f32[4,128]{1,0:T(4,128)S(1)} %log_add_fusion, bf16[4,128,128]{2,1,0:T(8,128)(2,1)S(1)} %get-tuple-element.81), kind=kOutput, calls=%fused_computation.12 | convolution fusion | flops 338165760 | bytes 10618880 | tf_op jit(solution)/shard_map/hgqjk,hgqd->hgjkd/dot_general | solution.py:185
  218.2 10.8 %scatter_fusion.1 = f32[13,128,128]{2,1,0:T(8,128)S(1)} fusion(f32[13,128,128]{2,1,0:T(8,128)S(1)} %broadcast.251.clone, s32[80]{0:T(128)S(1)} %reshape.413, f32[80,128,128]{2,1,0:T(8,128)} %bitcast.117), kind=kCustom, calls=%fused_computation.4 | custom fusion | flops 1310720 | bytes 15728960 | tf_op jit(solution)/shard_map/scatter-add | solution.py:189
  240.3 6.0 %all-to-all-start.1 = ((bf16[1,8,128,128]{3,2,0,1:T(8,128)(2,1)}), bf16[1,8,128,128]{3,2,0,1:T(8,128)(2,1)}, u32[]{:S(2)}, u32[]{:S(2)}) async-start(bf16[1,8,128,128]{3,2,0,1:T(8,128)(2,1)} %slice.51), calls=%async_computation.1 | async-start | bytes 524288 | tf_op jit(solution)/shard_map/all_to_all | solution.py:58
  247.6 10.8 %scatter_fusion = f32[13,128,128]{2,1,0:T(8,128)S(1)} fusion(f32[13,128,128]{2,1,0:T(8,128)S(1)} %broadcast.251.clone.1, s32[80]{0:T(128)S(1)} %reshape.413, f32[80,128,128]{2,1,0:T(8,128)} %bitcast.114), kind=kCustom, calls=%fused_computation.3 | custom fusion | flops 1310720 | bytes 15728960 | tf_op jit(solution)/shard_map/scatter-add | solution.py:188
  263.4 25.7 %psum.23 = f32[1,128]{1,0:T(1,128)} all-reduce(f32[1,128]{1,0:T(1,128)S(1)} %bitcast.151), channel_id=1, replica_groups=mesh['seq'=8,'head'=4] {'seq'}, use_global_device_ids=true, to_apply=%region_22.23 | all-reduce | flops 128 | bytes 1024 | tf_op jit(solution)/shard_map/psum | solution.py:141
  293.6 7.1 %all-to-all-done = bf16[1,8,128,128]{3,2,0,1:T(8,128)(2,1)S(1)} async-done(((bf16[1,8,128,128]{3,2,0,1:T(8,128)(2,1)}), bf16[1,8,128,128]{3,2,0,1:T(8,128)(2,1)S(1)}, u32[]{:S(2)}, u32[]{:S(2)}) %all-to-all-start) | async-done | bytes 262176 | tf_op jit(solution)/shard_map/all_to_all | solution.py:55
  (137 shorter events, 88.6 us)
Async XLA Ops:
  0.6 94.8 %copy-start = (bf16[1,512,128]{2,1,0:T(8,128)(2,1)S(1)}, bf16[1,512,128]{2,1,0:T(8,128)(2,1)}, u32[]{:S(2)}) copy-start(bf16[1,512,128]{2,1,0:T(8,128)(2,1)} %param.12) | copy-start | bytes 393220
  11.6 77.8 %collective-permute-start.3 = (bf16[1,1,128,128]{3,2,0,1:T(8,128)(2,1)S(1)}, bf16[1,1,128,128]{3,2,0,1:T(8,128)(2,1)S(1)}, u32[]{:S(2)}, u32[]{:S(2)}) collective-permute-start(bf16[1,1,128,128]{3,2,0,1:T(8,128)(2,1)S(1)} %get-tuple-element.68), channel_id=1, source_target_pairs={{0,4},{4,8},{8,12},{12,16},{16,20},{20,24},{24,28},{1,5},{5,9},{9,... | collective-permute-start | bytes 98312 | tf_op jit(solution)/shard_map/ppermute | solution.py:16
  17.8 73.6 %collective-permute-start.2 = (bf16[1,1,128,128]{3,2,0,1:T(8,128)(2,1)}, bf16[1,1,128,128]{3,2,0,1:T(8,128)(2,1)}, u32[]{:S(2)}, u32[]{:S(2)}) collective-permute-start(bf16[1,1,128,128]{3,2,0,1:T(8,128)(2,1)} %get-tuple-element.66), channel_id=1, source_target_pairs={{0,4},{4,8},{8,12},{12,16},{16,20},{20,24},{24,28},{1,5},{5,9},{9,... | collective-permute-start | bytes 98312 | tf_op jit(solution)/shard_map/ppermute | solution.py:16
  99.1 53.1 %copy-start.4 = (bf16[1,512,128]{2,1,0:T(8,128)(2,1)S(1)}, bf16[1,512,128]{2,1,0:T(8,128)(2,1)}, u32[]{:S(2)}) copy-start(bf16[1,512,128]{2,1,0:T(8,128)(2,1)} %param.18) | copy-start | bytes 393220
  99.1 53.1 %copy-start.11 = (f32[1,128]{1,0:T(1,128)S(1)}, f32[1,128]{1,0:T(1,128)}, u32[]{:S(2)}) copy-start(f32[1,128]{1,0:T(1,128)} %param.17) | copy-start | bytes 1540
  100.6 59.9 %copy-start.9 = (bf16[1,512,128]{2,1,0:T(8,128)(2,1)S(1)}, bf16[1,512,128]{2,1,0:T(8,128)(2,1)}, u32[]{:S(2)}) copy-start(bf16[1,512,128]{2,1,0:T(8,128)(2,1)} %param.15) | copy-start | bytes 393220
  101.3 3.2 %collective-permute-start = (f32[1,128,128]{2,1,0:T(8,128)S(1)}, f32[1,128,128]{2,1,0:T(8,128)S(1)}, u32[]{:S(2)}, u32[]{:S(2)}) collective-permute-start(f32[1,128,128]{2,1,0:T(8,128)S(1)} %add.214), channel_id=1, source_target_pairs={{0,4},{4,8},{8,12},{12,16},{16,20},{20,24},{24,28},{1,5},{5,9},{9,... | collective-permute-start | bytes 196616 | tf_op jit(solution)/shard_map/while/body/eval_jaxpr/ppermute | solution.py:16
  104.5 6.2 %collective-permute-start = (f32[1,128,128]{2,1,0:T(8,128)S(1)}, f32[1,128,128]{2,1,0:T(8,128)S(1)}, u32[]{:S(2)}, u32[]{:S(2)}) collective-permute-start(f32[1,128,128]{2,1,0:T(8,128)S(1)} %add.214), channel_id=1, source_target_pairs={{0,4},{4,8},{8,12},{12,16},{16,20},{20,24},{24,28},{1,5},{5,9},{9,... | collective-permute-start | bytes 196616 | tf_op jit(solution)/shard_map/while/body/eval_jaxpr/ppermute | solution.py:16
  110.7 6.2 %collective-permute-start = (f32[1,128,128]{2,1,0:T(8,128)S(1)}, f32[1,128,128]{2,1,0:T(8,128)S(1)}, u32[]{:S(2)}, u32[]{:S(2)}) collective-permute-start(f32[1,128,128]{2,1,0:T(8,128)S(1)} %add.214), channel_id=1, source_target_pairs={{0,4},{4,8},{8,12},{12,16},{16,20},{20,24},{24,28},{1,5},{5,9},{9,... | collective-permute-start | bytes 196616 | tf_op jit(solution)/shard_map/while/body/eval_jaxpr/ppermute | solution.py:16
  116.8 6.4 %collective-permute-start = (f32[1,128,128]{2,1,0:T(8,128)S(1)}, f32[1,128,128]{2,1,0:T(8,128)S(1)}, u32[]{:S(2)}, u32[]{:S(2)}) collective-permute-start(f32[1,128,128]{2,1,0:T(8,128)S(1)} %add.214), channel_id=1, source_target_pairs={{0,4},{4,8},{8,12},{12,16},{16,20},{20,24},{24,28},{1,5},{5,9},{9,... | collective-permute-start | bytes 196616 | tf_op jit(solution)/shard_map/while/body/eval_jaxpr/ppermute | solution.py:16
  123.3 7.3 %collective-permute-start = (f32[1,128,128]{2,1,0:T(8,128)S(1)}, f32[1,128,128]{2,1,0:T(8,128)S(1)}, u32[]{:S(2)}, u32[]{:S(2)}) collective-permute-start(f32[1,128,128]{2,1,0:T(8,128)S(1)} %add.214), channel_id=1, source_target_pairs={{0,4},{4,8},{8,12},{12,16},{16,20},{20,24},{24,28},{1,5},{5,9},{9,... | collective-permute-start | bytes 196616 | tf_op jit(solution)/shard_map/while/body/eval_jaxpr/ppermute | solution.py:16
  130.6 7.2 %collective-permute-start = (f32[1,128,128]{2,1,0:T(8,128)S(1)}, f32[1,128,128]{2,1,0:T(8,128)S(1)}, u32[]{:S(2)}, u32[]{:S(2)}) collective-permute-start(f32[1,128,128]{2,1,0:T(8,128)S(1)} %add.214), channel_id=1, source_target_pairs={{0,4},{4,8},{8,12},{12,16},{16,20},{20,24},{24,28},{1,5},{5,9},{9,... | collective-permute-start | bytes 196616 | tf_op jit(solution)/shard_map/while/body/eval_jaxpr/ppermute | solution.py:16
  137.8 7.1 %collective-permute-start = (f32[1,128,128]{2,1,0:T(8,128)S(1)}, f32[1,128,128]{2,1,0:T(8,128)S(1)}, u32[]{:S(2)}, u32[]{:S(2)}) collective-permute-start(f32[1,128,128]{2,1,0:T(8,128)S(1)} %add.214), channel_id=1, source_target_pairs={{0,4},{4,8},{8,12},{12,16},{16,20},{20,24},{24,28},{1,5},{5,9},{9,... | collective-permute-start | bytes 196616 | tf_op jit(solution)/shard_map/while/body/eval_jaxpr/ppermute | solution.py:16
  161.3 7.4 %collective-permute-start.1 = (f32[1,128,128]{2,1,0:T(8,128)S(1)}, f32[1,128,128]{2,1,0:T(8,128)S(1)}, u32[]{:S(2)}, u32[]{:S(2)}) collective-permute-start(f32[1,128,128]{2,1,0:T(8,128)S(1)} %add.216), channel_id=1, source_target_pairs={{4,0},{8,4},{12,8},{16,12},{20,16},{24,20},{28,24},{5,1},{9,5},{13... | collective-permute-start | bytes 196616 | tf_op jit(solution)/shard_map/while/body/eval_jaxpr/ppermute | solution.py:16
  168.7 7.4 %collective-permute-start.1 = (f32[1,128,128]{2,1,0:T(8,128)S(1)}, f32[1,128,128]{2,1,0:T(8,128)S(1)}, u32[]{:S(2)}, u32[]{:S(2)}) collective-permute-start(f32[1,128,128]{2,1,0:T(8,128)S(1)} %add.216), channel_id=1, source_target_pairs={{4,0},{8,4},{12,8},{16,12},{20,16},{24,20},{28,24},{5,1},{9,5},{13... | collective-permute-start | bytes 196616 | tf_op jit(solution)/shard_map/while/body/eval_jaxpr/ppermute | solution.py:16
  176.1 7.1 %collective-permute-start.1 = (f32[1,128,128]{2,1,0:T(8,128)S(1)}, f32[1,128,128]{2,1,0:T(8,128)S(1)}, u32[]{:S(2)}, u32[]{:S(2)}) collective-permute-start(f32[1,128,128]{2,1,0:T(8,128)S(1)} %add.216), channel_id=1, source_target_pairs={{4,0},{8,4},{12,8},{16,12},{20,16},{24,20},{28,24},{5,1},{9,5},{13... | collective-permute-start | bytes 196616 | tf_op jit(solution)/shard_map/while/body/eval_jaxpr/ppermute | solution.py:16
  183.2 7.1 %collective-permute-start.1 = (f32[1,128,128]{2,1,0:T(8,128)S(1)}, f32[1,128,128]{2,1,0:T(8,128)S(1)}, u32[]{:S(2)}, u32[]{:S(2)}) collective-permute-start(f32[1,128,128]{2,1,0:T(8,128)S(1)} %add.216), channel_id=1, source_target_pairs={{4,0},{8,4},{12,8},{16,12},{20,16},{24,20},{28,24},{5,1},{9,5},{13... | collective-permute-start | bytes 196616 | tf_op jit(solution)/shard_map/while/body/eval_jaxpr/ppermute | solution.py:16
  190.3 7.7 %collective-permute-start.1 = (f32[1,128,128]{2,1,0:T(8,128)S(1)}, f32[1,128,128]{2,1,0:T(8,128)S(1)}, u32[]{:S(2)}, u32[]{:S(2)}) collective-permute-start(f32[1,128,128]{2,1,0:T(8,128)S(1)} %add.216), channel_id=1, source_target_pairs={{4,0},{8,4},{12,8},{16,12},{20,16},{24,20},{28,24},{5,1},{9,5},{13... | collective-permute-start | bytes 196616 | tf_op jit(solution)/shard_map/while/body/eval_jaxpr/ppermute | solution.py:16
  197.9 6.8 %collective-permute-start.1 = (f32[1,128,128]{2,1,0:T(8,128)S(1)}, f32[1,128,128]{2,1,0:T(8,128)S(1)}, u32[]{:S(2)}, u32[]{:S(2)}) collective-permute-start(f32[1,128,128]{2,1,0:T(8,128)S(1)} %add.216), channel_id=1, source_target_pairs={{4,0},{8,4},{12,8},{16,12},{20,16},{24,20},{28,24},{5,1},{9,5},{13... | collective-permute-start | bytes 196616 | tf_op jit(solution)/shard_map/while/body/eval_jaxpr/ppermute | solution.py:16
  204.7 7.1 %collective-permute-start.1 = (f32[1,128,128]{2,1,0:T(8,128)S(1)}, f32[1,128,128]{2,1,0:T(8,128)S(1)}, u32[]{:S(2)}, u32[]{:S(2)}) collective-permute-start(f32[1,128,128]{2,1,0:T(8,128)S(1)} %add.216), channel_id=1, source_target_pairs={{4,0},{8,4},{12,8},{16,12},{20,16},{24,20},{28,24},{5,1},{9,5},{13... | collective-permute-start | bytes 196616 | tf_op jit(solution)/shard_map/while/body/eval_jaxpr/ppermute | solution.py:16
  240.3 48.8 %all-to-all-start.1 = ((bf16[1,8,128,128]{3,2,0,1:T(8,128)(2,1)}), bf16[1,8,128,128]{3,2,0,1:T(8,128)(2,1)}, u32[]{:S(2)}, u32[]{:S(2)}) async-start(bf16[1,8,128,128]{3,2,0,1:T(8,128)(2,1)} %slice.51), calls=%async_computation.1 | async-start | bytes 524288 | tf_op jit(solution)/shard_map/all_to_all | solution.py:58
  246.2 46.3 %collective-permute-start.5 = (bf16[1,1,128,128]{3,2,0,1:T(8,128)(2,1)}, bf16[1,1,128,128]{3,2,0,1:T(8,128)(2,1)S(1)}, u32[]{:S(2)}, u32[]{:S(2)}) collective-permute-start(bf16[1,1,128,128]{3,2,0,1:T(8,128)(2,1)} %slice.50), channel_id=1, source_target_pairs={{4,0},{8,4},{12,8},{16,12},{20,16},{24,20},{28,24},{5,1},{9,5},{13... | collective-permute-start | bytes 98312 | tf_op jit(solution)/shard_map/ppermute | solution.py:16
  258.6 34.0 %collective-permute-start.4 = (bf16[1,1,128,128]{3,2,0,1:T(8,128)(2,1)S(1)}, bf16[1,1,128,128]{3,2,0,1:T(8,128)(2,1)S(1)}, u32[]{:S(2)}, u32[]{:S(2)}) collective-permute-start(bf16[1,1,128,128]{3,2,0,1:T(8,128)(2,1)S(1)} %slice.47), channel_id=1, source_target_pairs={{4,0},{8,4},{12,8},{16,12},{20,16},{24,20},{28,24},{5,1},{9,5},{13... | collective-permute-start | bytes 98312 | tf_op jit(solution)/shard_map/ppermute | solution.py:16
  289.1 11.6 %all-to-all-start = ((bf16[1,8,128,128]{3,2,0,1:T(8,128)(2,1)}), bf16[1,8,128,128]{3,2,0,1:T(8,128)(2,1)S(1)}, u32[]{:S(2)}, u32[]{:S(2)}) async-start(bf16[1,8,128,128]{3,2,0,1:T(8,128)(2,1)} %slice.48), calls=%async_computation | async-start | bytes 524288 | tf_op jit(solution)/shard_map/all_to_all | solution.py:55
  (8 other events, 70.8 us)
where the time goes:
time: 303 us; the launch traced here: 302 us
  blocking collectives  102 us (34%)
  waiting for transfers between devices  61.6 us (20%)
  starting transfers between devices  60.1 us (20%)
  other arithmetic  37.4 us (12%)
  matrix products  27.5 us (9%)
  local copies, waits for them, and re-layouts  9.99 us (3%)
  between operations  3.08 us (1%)
    ppermute x18, waiting for transfers between devices, passed_along(): return lax.ppermute(value, axis, pairs)  54.5 us
    ppermute x18, starting transfers between devices, passed_along(): return lax.ppermute(value, axis, pairs)  50.7 us
    all_gather x1, blocking collectives, per_device(): lax.all_gather(own_key, 'seq', axis=1, tiled=True)  32.7 us
    all_gather x1, blocking collectives, per_device(): lax.all_gather(own_value, 'seq', axis=1, tiled=True)  30.8 us
    psum x1, blocking collectives, per_device(): grad_gain = lax.psum(jnp.sum(grad_out * normed, axis=(1, 2)), 'seq')  25.7 us
    scatter-add x1, other arithmetic, per_device(): grad_pool_value = grad_pool_value.at[:, slots].add(part_value)  10.8 us
    scatter-add x1, other arithmetic, per_device(): grad_pool_key = grad_pool_key.at[:, slots].add(part_key)  10.8 us
    all_to_all x1, waiting for transfers between devices, far_gradients(): lax.all_to_all(terms_key.astype(jnp.bfloat16), 'seq', split_axis=1, conca...  7.11 us
  transfers between devices with their start and end apart: 20, of which 15 were waited for; matrix products, arithmetic and copies ran while one was open for 8% of the time, Pallas kernels for 0%

commit v1 on v0

v1 whole, which is shorter than its diff:
```python
import functools

import jax
import jax.numpy as jnp
from jax import lax
from jax.experimental import pallas as pl
from jax.experimental.pallas import tpu as pltpu
from jax.sharding import PartitionSpec as P

BLK = 128
masked_value = -1e30
eps_norm = 1e-05
f32 = jnp.float32
bf16 = jnp.bfloat16
MESH = pl.DeviceIdType.MESH


def parts(x):
    if x.dtype == bf16:
        return (x,)
    high = x.astype(bf16)
    return (high, (x - high.astype(f32)).astype(bf16))


def dot(a, b, ca, cb):
    return lax.dot_general(a, b, (((ca,), (cb,)), ((), ())), preferred_element_type=f32)


def mm(a, b, ca, cb):
    pa, pb = parts(a), parts(b)
    out = None
    for i, x in enumerate(pa):
        for j, y in enumerate(pb):
            if i + j < 2:
                term = dot(x, y, ca, cb)
                out = term if out is None else out + term
    return out


def loop(low, high, body):
    def step(i, carry):
        body(i)
        return carry

    lax.fori_loop(low, high, step, jnp.int32(0))


def kernel(
    n, nh, scale,
    q, k, v, lq, lk, gain, cot, kbs, kbv,
    mixed, gq, gk, gv, glq, glk, gg,
    kvsend, kvbuf, kvext, stsend, stbuf, grsend, grbuf, hsend, hbuf, ggsend, ggbuf,
    gfsend, gfbuf, gbsend, gbbuf, att, wn, wf, dsf, pbf, mix,
    kv_s, kv_r, pv_s, pv_r, st_s, st_r, gr_s, gr_r, h_s, h_r, gg_s, gg_r, gf_s, gf_r, gb_s, gb_r,
):
    rows, width = q.shape
    blk = BLK
    per_dev = rows // blk
    me = lax.axis_index("seq")
    hd = lax.axis_index("head")
    features = nh * width

    barrier = pltpu.get_barrier_semaphore()

    def greet(d):
        pl.semaphore_signal(barrier, inc=1, device_id={"seq": d}, device_id_type=MESH)

    def greet_head(d):
        pl.semaphore_signal(barrier, inc=1, device_id={"head": d}, device_id_type=MESH)

    loop(0, me, greet)
    loop(me + 1, n, greet)
    loop(0, hd, greet_head)
    loop(hd + 1, nh, greet_head)

    def link(src, dst, ssem, rsem, axis, d):
        return pltpu.make_async_remote_copy(
            src_ref=src, dst_ref=dst, send_sem=ssem, recv_sem=rsem,
            device_id={axis: d}, device_id_type=MESH,
        )

    base = me * per_dev
    names = kbv[...]
    slot = lax.broadcasted_iota(jnp.int32, names.shape, 1)
    ours = (slot >= 2) & (names >= base) & (names < base + per_dev)
    local = jnp.where(ours, names - base, 0).astype(f32)
    mine = jnp.max(jnp.max(local, axis=1, keepdims=True), axis=0, keepdims=True)
    for side, ref in ((0, k), (1, v)):
        chosen = ref[0:blk, :].astype(f32)
        for g in range(1, per_dev):
            chosen = jnp.where(mine == g, ref[g * blk : (g + 1) * blk, :].astype(f32), chosen)
        kvsend[side] = chosen.astype(bf16)
        kvext[side, blk : blk + rows, :] = ref[...]

    pl.semaphore_wait(barrier, n - 1 + nh - 1)

    def kv_copy(slot_at, peer):
        return link(kvsend, kvbuf.at[:, slot_at], kv_s.at[peer], kv_r.at[slot_at], "seq", peer)

    def prev_copy(peer):
        return link(
            kvext.at[:, rows : rows + blk], kvext.at[:, 0:blk], pv_s, pv_r, "seq", peer
        )

    @pl.when(me < n - 1)
    def _():
        prev_copy(me + 1).start()

    loop(me + 1, n, lambda d: kv_copy(me, d).start())

    @pl.when(me == 0)
    def _():
        kvext[:, 0:blk, :] = jnp.zeros((2, blk, width), bf16)

    def clear(d):
        kvbuf[:, pl.ds(d, 1)] = jnp.zeros((2, 1, blk, width), bf16)

    loop(me, n, clear)

    tri = lax.broadcasted_iota(jnp.int32, (rows, rows), 0) >= lax.broadcasted_iota(
        jnp.int32, (rows, rows), 1
    )
    mix[...] = jnp.where(tri, dot(lq[...], lk[...], 1, 1), 0.0)

    @pl.when(me > 0)
    def _():
        prev_copy(me - 1).wait_recv()

    loop(0, me, lambda s: kv_copy(s, s).wait_recv())

    kfar = kvbuf[0].reshape(n * blk, width)
    vfar = kvbuf[1].reshape(n * blk, width)

    row_i = lax.broadcasted_iota(jnp.int32, (blk, 2 * blk), 0)
    col_i = lax.broadcasted_iota(jnp.int32, (blk, 2 * blk), 1)
    causal = (col_i >= blk) & (col_i - blk <= row_i)
    first = lax.broadcasted_iota(jnp.int32, (1, n * blk), 1) // blk * per_dev
    inv_total = []
    for g in range(per_dev):
        at = slice(g * blk, (g + 1) * blk)
        near = slice(g * blk, (g + 2) * blk)
        qg = q[at, :]
        reach = blk if g else jnp.where(me > 0, blk, 0)
        sn = jnp.where(causal | (col_i < reach), dot(qg, kvext[0, near, :], 1, 1) * scale, masked_value)
        hit = jnp.zeros((1, n * blk), jnp.int32)
        for j in range(2, kbs.shape[1]):
            name = kbs[base + g, j]
            hit = jnp.maximum(
                hit, jnp.where((first <= name) & (name < first + per_dev), 1, 0)
            )
        sf = jnp.where(hit > 0, dot(qg, kfar, 1, 1) * scale, masked_value)
        top = jnp.maximum(
            jnp.max(sn, axis=1, keepdims=True), jnp.max(sf, axis=1, keepdims=True)
        )
        en = jnp.exp(sn - top)
        ef = jnp.exp(sf - top)
        total = jnp.sum(en, axis=1, keepdims=True) + jnp.sum(ef, axis=1, keepdims=True)
        summed = dot(en.astype(bf16), kvext[1, near, :], 1, 0) + dot(ef.astype(bf16), vfar, 1, 0)
        att[at, :] = (summed / total).astype(bf16)
        wn[at, :] = en
        wf[at, :] = ef
        inv_total.append(1.0 / total)

    stsend[...] = dot(lk[...], att[...], 0, 0)

    def st_copy(slot_at, peer):
        return link(stsend, stbuf.at[slot_at], st_s.at[peer], st_r.at[slot_at], "seq", peer)

    loop(me + 1, n, lambda d: st_copy(me, d).start())
    linear = mm(mix[...], att[...], 1, 0)

    def take_state(s, acc):
        st_copy(s, s).wait_recv()
        return acc + stbuf[s]

    prior = lax.fori_loop(0, me, take_state, jnp.zeros((width, width), f32))
    linear = linear + mm(lq[...], prior, 1, 0)
    co = cot[...].astype(f32)
    scaled = co * gain[...]
    ones = jnp.ones((8, width), bf16)
    hsend[0:8, :] = mm(ones, linear * linear, 1, 1)
    hsend[8:16, :] = mm(ones, scaled * linear, 1, 1)

    def h_copy(slot_at, peer):
        return link(hsend, hbuf.at[slot_at], h_s.at[peer], h_r.at[slot_at], "head", peer)

    loop(0, hd, lambda d: h_copy(hd, d).start())
    loop(hd + 1, nh, lambda d: h_copy(hd, d).start())

    def take_head(s, acc):
        h_copy(s, s).wait_recv()
        return acc + hbuf[s]

    heads = lax.fori_loop(0, hd, take_head, hsend[...])
    heads = lax.fori_loop(hd + 1, nh, take_head, heads)
    spread = jnp.full((8, width), 0.125, bf16)
    squares = mm(heads[0:8, :], spread, 0, 0)
    crossed = mm(heads[8:16, :], spread, 0, 0)
    inv_rms = lax.rsqrt(squares / features + eps_norm)
    normed = linear * inv_rms
    a32 = att[...].astype(f32)
    grad_linear = inv_rms * (scaled - normed * (crossed * inv_rms / features))

    grsend[...] = mm(lq[...], grad_linear, 0, 0)

    def gr_copy(slot_at, peer):
        return link(grsend, grbuf.at[slot_at], gr_s.at[peer], gr_r.at[slot_at], "seq", peer)

    loop(0, me, lambda d: gr_copy(me, d).start())
    ggsend[...] = jnp.broadcast_to(jnp.sum(co * normed, axis=0, keepdims=True), (8, width))

    def gg_copy(slot_at, peer):
        return link(ggsend, ggbuf.at[slot_at], gg_s.at[peer], gg_r.at[slot_at], "seq", peer)

    loop(0, me, lambda d: gg_copy(me, d).start())
    loop(me + 1, n, lambda d: gg_copy(me, d).start())

    mixed[...] = (a32 + gain[...] * normed).astype(bf16)
    pairs = jnp.where(tri, mm(grad_linear, att[...], 1, 1), 0.0)
    glq[...] = (mm(pairs, lk[...], 1, 0) + mm(grad_linear, prior, 1, 1)).astype(bf16)
    grad_lk = mm(pairs, lq[...], 0, 0)
    grad_att = co + mm(mix[...], grad_linear, 0, 0)

    def take_grad(s, acc):
        gr_copy(s, s).wait_recv()
        return acc + grbuf[s]

    later = lax.fori_loop(me + 1, n, take_grad, jnp.zeros((width, width), f32))
    glk[...] = (grad_lk + mm(att[...], later, 1, 1)).astype(bf16)
    grad_att = (grad_att + mm(lk[...], later, 1, 0)).astype(bf16)
    delta = jnp.sum(grad_att.astype(f32) * a32, axis=1, keepdims=True)

    for g in range(per_dev):
        at = slice(g * blk, (g + 1) * blk)
        pf = wf[at, :] * inv_total[g]
        pbf[at, :] = pf.astype(bf16)
        dsf[at, :] = (pf * (dot(grad_att[at, :], vfar, 1, 1) - delta[at, :])).astype(bf16)
    gfsend[0] = (dot(dsf[...], q[...], 0, 0) * scale).astype(bf16).reshape(n, blk, width)
    gfsend[1] = dot(pbf[...], grad_att, 0, 0).astype(bf16).reshape(n, blk, width)

    def gf_copy(slot_at, peer):
        return link(
            gfsend.at[:, peer], gfbuf.at[:, slot_at], gf_s.at[peer], gf_r.at[slot_at], "seq", peer
        )

    loop(0, me, lambda d: gf_copy(me, d).start())

    key_terms = [None] * (per_dev + 1)
    value_terms = [None] * (per_dev + 1)

    def put(terms, i, x):
        terms[i] = x if terms[i] is None else terms[i] + x

    def gb_copy(peer):
        return link(gbsend, gbbuf, gb_s, gb_r, "seq", peer)

    for g in range(per_dev):
        at = slice(g * blk, (g + 1) * blk)
        near = slice(g * blk, (g + 2) * blk)
        pn = wn[at, :] * inv_total[g]
        ga = grad_att[at, :]
        ds = (pn * (dot(ga, kvext[1, near, :], 1, 1) - delta[at, :])).astype(bf16)
        nk = dot(ds, q[at, :], 0, 0) * scale
        nv = dot(pn.astype(bf16), ga, 0, 0)
        for i in range(2):
            half = slice(i * blk, (i + 1) * blk)
            put(key_terms, g + i, nk[half, :])
            put(value_terms, g + i, nv[half, :])
        if g == 0:
            gbsend[0] = key_terms[0].astype(bf16)
            gbsend[1] = value_terms[0].astype(bf16)

            @pl.when(me > 0)
            def _():
                gb_copy(me - 1).start()

        gq[at, :] = (
            (dot(ds, kvext[0, near, :], 1, 0) + dot(dsf[at, :], kfar, 1, 0)) * scale
        ).astype(bf16)

    def take_gain(s, acc):
        gg_copy(s, s).wait_recv()
        return acc + ggbuf[s]

    gains = lax.fori_loop(0, me, take_gain, ggsend[...])
    gains = lax.fori_loop(me + 1, n, take_gain, gains)
    gg[...] = gains[0:1, :]

    @pl.when(me == n - 1)
    def _():
        gbbuf[...] = jnp.zeros_like(gbbuf)

    @pl.when(me < n - 1)
    def _():
        gb_copy(me + 1).wait_recv()

    zero = jnp.zeros((blk, width), f32)

    def take_far(s, acc):
        gf_copy(s, s).wait_recv()
        return (acc[0] + gfbuf[0, s].astype(f32), acc[1] + gfbuf[1, s].astype(f32))

    far = lax.fori_loop(me + 1, n, take_far, (zero, zero))
    for side, (terms, out) in enumerate(((key_terms, gk), (value_terms, gv))):
        for g in range(per_dev):
            x = terms[g + 1] + jnp.where(mine == g, far[side], 0.0)
            if g == per_dev - 1:
                x = x + gbbuf[side].astype(f32)
            out[g * blk : (g + 1) * blk, :] = x.astype(bf16)

    @pl.when(me < n - 1)
    def _():
        prev_copy(me + 1).wait_send()

    @pl.when(me > 0)
    def _():
        gb_copy(me - 1).wait_send()

    def sent_up(d):
        kv_copy(me, d).wait_send()
        st_copy(me, d).wait_send()
        gg_copy(me, d).wait_send()

    def sent_down(d):
        gr_copy(me, d).wait_send()
        gf_copy(me, d).wait_send()
        gg_copy(me, d).wait_send()

    loop(me + 1, n, sent_up)
    loop(0, me, sent_down)
    loop(0, hd, lambda d: h_copy(hd, d).wait_send())
    loop(hd + 1, nh, lambda d: h_copy(hd, d).wait_send())


def per_device(query, key, value, lin_query, lin_key, gain, cotangent, key_block):
    heads, rows, width = query.shape
    n = lax.axis_size("seq")
    nh = lax.axis_size("head")
    blk = BLK
    flat = lambda x: x.reshape(heads * rows, width)
    vm = pl.BlockSpec(memory_space=pltpu.VMEM)
    big = jax.ShapeDtypeStruct((rows, width), bf16)
    dma = pltpu.SemaphoreType.DMA
    outs = pl.pallas_call(
        functools.partial(kernel, n, nh, width ** (-0.5)),
        out_shape=[big] * 6 + [jax.ShapeDtypeStruct((1, width), f32)],
        in_specs=[vm] * 7 + [pl.BlockSpec(memory_space=pltpu.SMEM), vm],
        out_specs=[vm] * 7,
        scratch_shapes=[
            pltpu.VMEM((2, blk, width), bf16),
            pltpu.VMEM((2, n, blk, width), bf16),
            pltpu.VMEM((2, rows + blk, width), bf16),
            pltpu.VMEM((width, width), f32),
            pltpu.VMEM((n, width, width), f32),
            pltpu.VMEM((width, width), f32),
            pltpu.VMEM((n, width, width), f32),
            pltpu.VMEM((16, rows), f32),
            pltpu.VMEM((nh, 16, rows), f32),
            pltpu.VMEM((8, width), f32),
            pltpu.VMEM((n, 8, width), f32),
            pltpu.VMEM((2, n, blk, width), bf16),
            pltpu.VMEM((2, n, blk, width), bf16),
            pltpu.VMEM((2, blk, width), bf16),
            pltpu.VMEM((2, blk, width), bf16),
            pltpu.VMEM((rows, width), bf16),
            pltpu.VMEM((rows, 2 * blk), f32),
            pltpu.VMEM((rows, n * blk), f32),
            pltpu.VMEM((rows, n * blk), bf16),
            pltpu.VMEM((rows, n * blk), bf16),
            pltpu.VMEM((rows, rows), f32),
            dma((n,)), dma((n,)), dma, dma,
            dma((n,)), dma((n,)), dma((n,)), dma((n,)),
            dma((nh,)), dma((nh,)), dma((n,)), dma((n,)),
            dma((n,)), dma((n,)), dma, dma,
        ],
        compiler_params=pltpu.CompilerParams(
            collective_id=0, has_side_effects=True, vmem_limit_bytes=56 * 2**20
        ),
    )(
        flat(query), flat(key), flat(value), flat(lin_query), flat(lin_key), gain,
        flat(cotangent), key_block, key_block,
    )
    return tuple(x.reshape(heads, rows, width) for x in outs[:6]) + (outs[6],)


def solution(mesh):
    split = P("head", "seq", None)
    return jax.shard_map(
        per_device,
        mesh=mesh,
        in_specs=(split,) * 5 + (P("head", None), split, P()),
        out_specs=(split,) * 6 + (P("head", None),),
        check_vma=False,
    )
```

time: 303 us -> 70.3 us (0.23)
  the two profiles are of different devices: /device:TPU:0 before, /device:TPU:11 now
where the time goes in v1:
time: 70.3 us; the launch traced here: 70 us
  Pallas kernels  61.4 us (87%)
  local copies, waits for them, and re-layouts  7.97 us (11%)
    pallas_call x1, Pallas kernels, per_device(): pl.pallas_call(functools.partial(kernel, n, nh, width ** (-0.5)), out_sha...  61.4 us
    unnamed x20, local copies, waits for them, and re-layouts  7.97 us

profile of v1, /device:TPU:11, one launch (start us, length us, event | category | flops | bytes accessed | tf_op | source)
XLA Modules:
  0.0 70.0 jit_solution(3410693563526848006)
XLA Ops:
  0.6 1.4 %copy.15.kbs.kbv = s32[32,20]{1,0:T(8,128)} copy(s32[32,20]{0,1:T(8,128)} %param.15) | data formatting | bytes 5120 | tf_op args[7]
  2.0 61.4 %shard_map.135 = (bf16[512,128]{1,0:T(8,128)(2,1)}, bf16[512,128]{1,0:T(8,128)(2,1)}, bf16[512,128]{1,0:T(8,128)(2,1)}, bf16[512,128]{1,0:T(8,128)(2,1)}, bf16[5...) custom-call(bf16[512,128]{1,0:T(8,128)(2,1)} %bitcast.18, bf16[512,128]{1,0:T(8,128)(2,1)} %bitcast.19, ...), custom_call_target="tpu_custom_call" | custom-call | tf_op jit(solution)/shard_map/pallas_call | solution.py:344
  63.4 0.0 copy-start.4
  63.4 1.6 %copy.24 = bf16[1,512,128]{2,1,0:T(8,128)(2,1)} copy(bf16[1,512,128]{2,1,0:T(8,128)(2,1)} %bitcast.17) | data formatting | bytes 262144
  65.0 0.0 copy-done.4
  65.0 0.0 copy-start.3
  65.0 0.7 copy.25
  65.7 0.3 copy-done.3
  66.0 0.0 copy-start.2
  66.0 0.7 copy.26
  66.6 0.3 copy-done.2
  66.9 0.0 copy-start.1
  66.9 0.7 copy.27
  67.6 0.3 copy-done.1
  67.9 0.0 copy-start
  67.9 0.7 copy.28
  68.5 0.3 copy-done
  68.8 0.0 copy-start.5
  68.8 0.7 copy.29
  69.5 0.0 copy-done.5
  69.5 0.5 copy.30
Async XLA Ops:
  63.4 1.6 %copy-start.4 = (bf16[512,128]{1,0:T(8,128)(2,1)S(1)}, bf16[512,128]{1,0:T(8,128)(2,1)}, u32[]{:S(2)}) copy-start(bf16[512,128]{1,0:T(8,128)(2,1)} %get-tuple-element.15) | copy-start | bytes 393220
  65.0 1.0 %copy-start.3 = (bf16[512,128]{1,0:T(8,128)(2,1)S(1)}, bf16[512,128]{1,0:T(8,128)(2,1)}, u32[]{:S(2)}) copy-start(bf16[512,128]{1,0:T(8,128)(2,1)} %get-tuple-element.16) | copy-start | bytes 393220
  66.0 1.0 %copy-start.2 = (bf16[512,128]{1,0:T(8,128)(2,1)S(1)}, bf16[512,128]{1,0:T(8,128)(2,1)}, u32[]{:S(2)}) copy-start(bf16[512,128]{1,0:T(8,128)(2,1)} %get-tuple-element.17) | copy-start | bytes 393220
  66.9 1.0 %copy-start.1 = (bf16[512,128]{1,0:T(8,128)(2,1)S(1)}, bf16[512,128]{1,0:T(8,128)(2,1)}, u32[]{:S(2)}) copy-start(bf16[512,128]{1,0:T(8,128)(2,1)} %get-tuple-element.18) | copy-start | bytes 393220
  67.9 1.0 %copy-start = (bf16[512,128]{1,0:T(8,128)(2,1)S(1)}, bf16[512,128]{1,0:T(8,128)(2,1)}, u32[]{:S(2)}) copy-start(bf16[512,128]{1,0:T(8,128)(2,1)} %get-tuple-element.19) | copy-start | bytes 393220
  68.8 0.7 copy-start.5

commit v2 on v1

--- a/solution.py
+++ b/solution.py
@@ -48,7 +48,7 @@
 def kernel(
     n, nh, scale,
     q, k, v, lq, lk, gain, cot, kbs, kbv,
-    mixed, gq, gk, gv, glq, glk, gg,
+    out, gg,
     kvsend, kvbuf, kvext, stsend, stbuf, grsend, grbuf, hsend, hbuf, ggsend, ggbuf,
     gfsend, gfbuf, gbsend, gbbuf, att, wn, wf, dsf, pbf, mix,
     kv_s, kv_r, pv_s, pv_r, st_s, st_r, gr_s, gr_r, h_s, h_r, gg_s, gg_r, gf_s, gf_r, gb_s, gb_r,
@@ -59,6 +59,7 @@
     me = lax.axis_index("seq")
     hd = lax.axis_index("head")
     features = nh * width
+    mixed, gq, gk, gv, glq, glk = (out.at[i] for i in range(6))
 
     barrier = pltpu.get_barrier_semaphore()
 
@@ -81,7 +82,7 @@
 
     base = me * per_dev
     names = kbv[...]
-    slot = lax.broadcasted_iota(jnp.int32, names.shape, 1)
+    slot = lax.broadcasted_iota(jnp.int32, names.shape, 0)
     ours = (slot >= 2) & (names >= base) & (names < base + per_dev)
     local = jnp.where(ours, names - base, 0).astype(f32)
     mine = jnp.max(jnp.max(local, axis=1, keepdims=True), axis=0, keepdims=True)
@@ -94,8 +95,11 @@
 
     pl.semaphore_wait(barrier, n - 1 + nh - 1)
 
-    def kv_copy(slot_at, peer):
-        return link(kvsend, kvbuf.at[:, slot_at], kv_s.at[peer], kv_r.at[slot_at], "seq", peer)
+    def kv_copy(side, slot_at, peer):
+        return link(
+            kvsend.at[side], kvbuf.at[side, slot_at], kv_s.at[side, peer], kv_r.at[side, slot_at],
+            "seq", peer,
+        )
 
     def prev_copy(peer):
         return link(
@@ -106,7 +110,8 @@
     def _():
         prev_copy(me + 1).start()
 
-    loop(me + 1, n, lambda d: kv_copy(me, d).start())
+    loop(0, n - 1 - me, lambda i: kv_copy(0, me, n - 1 - i).start())
+    loop(0, n - 1 - me, lambda i: kv_copy(1, me, n - 1 - i).start())
 
     @pl.when(me == 0)
     def _():
@@ -122,64 +127,82 @@
     )
     mix[...] = jnp.where(tri, dot(lq[...], lk[...], 1, 1), 0.0)
 
-    @pl.when(me > 0)
-    def _():
-        prev_copy(me - 1).wait_recv()
-
-    loop(0, me, lambda s: kv_copy(s, s).wait_recv())
-
-    kfar = kvbuf[0].reshape(n * blk, width)
-    vfar = kvbuf[1].reshape(n * blk, width)
-
     row_i = lax.broadcasted_iota(jnp.int32, (blk, 2 * blk), 0)
     col_i = lax.broadcasted_iota(jnp.int32, (blk, 2 * blk), 1)
     causal = (col_i >= blk) & (col_i - blk <= row_i)
+
+    def near_scores(g):
+        at = slice(g * blk, (g + 1) * blk)
+        near = slice(g * blk, (g + 2) * blk)
+        reach = blk if g else jnp.where(me > 0, blk, 0)
+        wn[at, :] = jnp.where(
+            causal | (col_i < reach), dot(q[at, :], kvext[0, near, :], 1, 1) * scale, masked_value
+        )
+
+    for g in range(1, per_dev):
+        near_scores(g)
+
+    @pl.when(me > 0)
+    def _():
+        prev_copy(me - 1).wait_recv()
+
+    near_scores(0)
+    loop(0, me, lambda s: kv_copy(0, s, s).wait_recv())
+    kfar = kvbuf[0].reshape(n * blk, width)
     first = lax.broadcasted_iota(jnp.int32, (1, n * blk), 1) // blk * per_dev
     inv_total = []
+    near_sum = []
     for g in range(per_dev):
         at = slice(g * blk, (g + 1) * blk)
         near = slice(g * blk, (g + 2) * blk)
-        qg = q[at, :]
-        reach = blk if g else jnp.where(me > 0, blk, 0)
-        sn = jnp.where(causal | (col_i < reach), dot(qg, kvext[0, near, :], 1, 1) * scale, masked_value)
         hit = jnp.zeros((1, n * blk), jnp.int32)
-        for j in range(2, kbs.shape[1]):
-            name = kbs[base + g, j]
+        for j in range(2, kbs.shape[0]):
+            name = kbs[j, base + g]
             hit = jnp.maximum(
                 hit, jnp.where((first <= name) & (name < first + per_dev), 1, 0)
             )
-        sf = jnp.where(hit > 0, dot(qg, kfar, 1, 1) * scale, masked_value)
+        sn = wn[at, :]
+        sf = jnp.where(hit > 0, dot(q[at, :], kfar, 1, 1) * scale, masked_value)
         top = jnp.maximum(
             jnp.max(sn, axis=1, keepdims=True), jnp.max(sf, axis=1, keepdims=True)
         )
         en = jnp.exp(sn - top)
         ef = jnp.exp(sf - top)
         total = jnp.sum(en, axis=1, keepdims=True) + jnp.sum(ef, axis=1, keepdims=True)
-        summed = dot(en.astype(bf16), kvext[1, near, :], 1, 0) + dot(ef.astype(bf16), vfar, 1, 0)
-        att[at, :] = (summed / total).astype(bf16)
+        inv_total.append(1.0 / total)
+        near_sum.append(dot(en.astype(bf16), kvext[1, near, :], 1, 0))
         wn[at, :] = en
         wf[at, :] = ef
-        inv_total.append(1.0 / total)
-
-    stsend[...] = dot(lk[...], att[...], 0, 0)
+        pbf[at, :] = ef.astype(bf16)
+
+    loop(0, me, lambda s: kv_copy(1, s, s).wait_recv())
+    vfar = kvbuf[1].reshape(n * blk, width)
+    far_sum = dot(pbf[...], vfar, 1, 0)
+    for g in range(per_dev):
+        at = slice(g * blk, (g + 1) * blk)
+        att[at, :] = ((near_sum[g] + far_sum[at, :]) * inv_total[g]).astype(bf16)
+
+    stsend[...] = dot(lk[...], att[...], 0, 0).astype(bf16)
 
     def st_copy(slot_at, peer):
         return link(stsend, stbuf.at[slot_at], st_s.at[peer], st_r.at[slot_at], "seq", peer)
 
-    loop(me + 1, n, lambda d: st_copy(me, d).start())
+    loop(0, n - 1 - me, lambda i: st_copy(me, n - 1 - i).start())
     linear = mm(mix[...], att[...], 1, 0)
 
     def take_state(s, acc):
         st_copy(s, s).wait_recv()
-        return acc + stbuf[s]
+        return acc + stbuf[s].astype(f32)
 
     prior = lax.fori_loop(0, me, take_state, jnp.zeros((width, width), f32))
     linear = linear + mm(lq[...], prior, 1, 0)
     co = cot[...].astype(f32)
     scaled = co * gain[...]
     ones = jnp.ones((8, width), bf16)
-    hsend[0:8, :] = mm(ones, linear * linear, 1, 1)
-    hsend[8:16, :] = mm(ones, scaled * linear, 1, 1)
+    upper = lax.broadcasted_iota(jnp.int32, (8, 1), 0) < 4
+    hsend[...] = jnp.where(
+        upper, mm(ones, linear * linear, 1, 1), mm(ones, scaled * linear, 1, 1)
+    )
 
     def h_copy(slot_at, peer):
         return link(hsend, hbuf.at[slot_at], h_s.at[peer], h_r.at[slot_at], "head", peer)
@@ -193,15 +216,15 @@
 
     heads = lax.fori_loop(0, hd, take_head, hsend[...])
     heads = lax.fori_loop(hd + 1, nh, take_head, heads)
-    spread = jnp.full((8, width), 0.125, bf16)
-    squares = mm(heads[0:8, :], spread, 0, 0)
-    crossed = mm(heads[8:16, :], spread, 0, 0)
+    half = lax.broadcasted_iota(jnp.int32, (8, width), 0) < 4
+    squares = mm(heads, jnp.where(half, 0.25, 0.0).astype(bf16), 0, 0)
+    crossed = mm(heads, jnp.where(half, 0.0, 0.25).astype(bf16), 0, 0)
     inv_rms = lax.rsqrt(squares / features + eps_norm)
     normed = linear * inv_rms
     a32 = att[...].astype(f32)
     grad_linear = inv_rms * (scaled - normed * (crossed * inv_rms / features))
 
-    grsend[...] = mm(lq[...], grad_linear, 0, 0)
+    grsend[...] = mm(lq[...], grad_linear, 0, 0).astype(bf16)
 
     def gr_copy(slot_at, peer):
         return link(grsend, grbuf.at[slot_at], gr_s.at[peer], gr_r.at[slot_at], "seq", peer)
@@ -215,35 +238,37 @@
     loop(0, me, lambda d: gg_copy(me, d).start())
     loop(me + 1, n, lambda d: gg_copy(me, d).start())
 
-    mixed[...] = (a32 + gain[...] * normed).astype(bf16)
+    grad_att = co + mm(mix[...], grad_linear, 0, 0)
     pairs = jnp.where(tri, mm(grad_linear, att[...], 1, 1), 0.0)
+    mix[...] = pairs
     glq[...] = (mm(pairs, lk[...], 1, 0) + mm(grad_linear, prior, 1, 1)).astype(bf16)
-    grad_lk = mm(pairs, lq[...], 0, 0)
-    grad_att = co + mm(mix[...], grad_linear, 0, 0)
+    for g in range(per_dev):
+        at = slice(g * blk, (g + 1) * blk)
+        pf = wf[at, :] * inv_total[g]
+        wf[at, :] = pf
+        pbf[at, :] = pf.astype(bf16)
 
     def take_grad(s, acc):
         gr_copy(s, s).wait_recv()
-        return acc + grbuf[s]
+        return acc + grbuf[s].astype(f32)
 
     later = lax.fori_loop(me + 1, n, take_grad, jnp.zeros((width, width), f32))
-    glk[...] = (grad_lk + mm(att[...], later, 1, 1)).astype(bf16)
     grad_att = (grad_att + mm(lk[...], later, 1, 0)).astype(bf16)
     delta = jnp.sum(grad_att.astype(f32) * a32, axis=1, keepdims=True)
 
+    def gf_copy(side, slot_at, peer):
+        return link(
+            gfsend.at[side, peer], gfbuf.at[side, slot_at], gf_s.at[side, peer],
+            gf_r.at[side, slot_at], "seq", peer,
+        )
+
+    gfsend[1] = dot(pbf[...], grad_att, 0, 0).astype(bf16).reshape(n, blk, width)
+    loop(0, me, lambda d: gf_copy(1, me, d).start())
     for g in range(per_dev):
         at = slice(g * blk, (g + 1) * blk)
-        pf = wf[at, :] * inv_total[g]
-        pbf[at, :] = pf.astype(bf16)
-        dsf[at, :] = (pf * (dot(grad_att[at, :], vfar, 1, 1) - delta[at, :])).astype(bf16)
+        dsf[at, :] = (wf[at, :] * (dot(grad_att[at, :], vfar, 1, 1) - delta[at, :])).astype(bf16)
     gfsend[0] = (dot(dsf[...], q[...], 0, 0) * scale).astype(bf16).reshape(n, blk, width)
-    gfsend[1] = dot(pbf[...], grad_att, 0, 0).astype(bf16).reshape(n, blk, width)
-
-    def gf_copy(slot_at, peer):
-        return link(
-            gfsend.at[:, peer], gfbuf.at[:, slot_at], gf_s.at[peer], gf_r.at[slot_at], "seq", peer
-        )
-
-    loop(0, me, lambda d: gf_copy(me, d).start())
+    loop(0, me, lambda d: gf_copy(0, me, d).start())
 
     key_terms = [None] * (per_dev + 1)
     value_terms = [None] * (per_dev + 1)
@@ -278,6 +303,9 @@
             (dot(ds, kvext[0, near, :], 1, 0) + dot(dsf[at, :], kfar, 1, 0)) * scale
         ).astype(bf16)
 
+    glk[...] = (mm(mix[...], lq[...], 0, 0) + mm(att[...], later, 1, 1)).astype(bf16)
+    mixed[...] = (a32 + gain[...] * normed).astype(bf16)
+
     def take_gain(s, acc):
         gg_copy(s, s).wait_recv()
         return acc + ggbuf[s]
@@ -296,17 +324,18 @@
 
     zero = jnp.zeros((blk, width), f32)
 
-    def take_far(s, acc):
-        gf_copy(s, s).wait_recv()
-        return (acc[0] + gfbuf[0, s].astype(f32), acc[1] + gfbuf[1, s].astype(f32))
-
-    far = lax.fori_loop(me + 1, n, take_far, (zero, zero))
-    for side, (terms, out) in enumerate(((key_terms, gk), (value_terms, gv))):
+    for side, terms, result in ((1, value_terms, gv), (0, key_terms, gk)):
+
+        def take_far(s, acc):
+            gf_copy(side, s, s).wait_recv()
+            return acc + gfbuf[side, s].astype(f32)
+
+        far = lax.fori_loop(me + 1, n, take_far, zero)
         for g in range(per_dev):
-            x = terms[g + 1] + jnp.where(mine == g, far[side], 0.0)
+            x = terms[g + 1] + jnp.where(mine == g, far, 0.0)
             if g == per_dev - 1:
                 x = x + gbbuf[side].astype(f32)
-            out[g * blk : (g + 1) * blk, :] = x.astype(bf16)
+            result[g * blk : (g + 1) * blk, :] = x.astype(bf16)
 
     @pl.when(me < n - 1)
     def _():
@@ -317,19 +346,33 @@
         gb_copy(me - 1).wait_send()
 
     def sent_up(d):
-        kv_copy(me, d).wait_send()
+        kv_copy(0, me, d).wait_send()
+        kv_copy(1, me, d).wait_send()
         st_copy(me, d).wait_send()
         gg_copy(me, d).wait_send()
 
     def sent_down(d):
         gr_copy(me, d).wait_send()
-        gf_copy(me, d).wait_send()
+        gf_copy(0, me, d).wait_send()
+        gf_copy(1, me, d).wait_send()
         gg_copy(me, d).wait_send()
 
     loop(me + 1, n, sent_up)
     loop(0, me, sent_down)
     loop(0, hd, lambda d: h_copy(hd, d).wait_send())
     loop(hd + 1, nh, lambda d: h_copy(hd, d).wait_send())
+
+
+def hand_out(stacked, gains, *refs):
+    sems = refs[7]
+    copies = [
+        pltpu.make_async_copy(stacked.at[pl.ds(i, 1)], refs[i], sems.at[i]) for i in range(6)
+    ]
+    copies.append(pltpu.make_async_copy(gains, refs[6], sems.at[6]))
+    for copy in copies:
+        copy.start()
+    for copy in copies:
+        copy.wait()
 
 
 def per_device(query, key, value, lin_query, lin_key, gain, cotangent, key_block):
@@ -339,23 +382,24 @@
     blk = BLK
     flat = lambda x: x.reshape(heads * rows, width)
     vm = pl.BlockSpec(memory_space=pltpu.VMEM)
-    big = jax.ShapeDtypeStruct((rows, width), bf16)
+    hbm = pl.BlockSpec(memory_space=pl.ANY)
+    total = jax.ShapeDtypeStruct((1, width), f32)
     dma = pltpu.SemaphoreType.DMA
-    outs = pl.pallas_call(
+    stacked, gains = pl.pallas_call(
         functools.partial(kernel, n, nh, width ** (-0.5)),
-        out_shape=[big] * 6 + [jax.ShapeDtypeStruct((1, width), f32)],
+        out_shape=[jax.ShapeDtypeStruct((6, rows, width), bf16), total],
         in_specs=[vm] * 7 + [pl.BlockSpec(memory_space=pltpu.SMEM), vm],
-        out_specs=[vm] * 7,
+        out_specs=[vm] * 2,
         scratch_shapes=[
             pltpu.VMEM((2, blk, width), bf16),
             pltpu.VMEM((2, n, blk, width), bf16),
             pltpu.VMEM((2, rows + blk, width), bf16),
-            pltpu.VMEM((width, width), f32),
-            pltpu.VMEM((n, width, width), f32),
-            pltpu.VMEM((width, width), f32),
-            pltpu.VMEM((n, width, width), f32),
-            pltpu.VMEM((16, rows), f32),
-            pltpu.VMEM((nh, 16, rows), f32),
+            pltpu.VMEM((width, width), bf16),
+            pltpu.VMEM((n, width, width), bf16),
+            pltpu.VMEM((width, width), bf16),
+            pltpu.VMEM((n, width, width), bf16),
+            pltpu.VMEM((8, rows), f32),
+            pltpu.VMEM((nh, 8, rows), f32),
             pltpu.VMEM((8, width), f32),
             pltpu.VMEM((n, 8, width), f32),
             pltpu.VMEM((2, n, blk, width), bf16),
@@ -368,19 +412,27 @@
             pltpu.VMEM((rows, n * blk), bf16),
             pltpu.VMEM((rows, n * blk), bf16),
             pltpu.VMEM((rows, rows), f32),
-            dma((n,)), dma((n,)), dma, dma,
+            dma((2, n)), dma((2, n)), dma, dma,
             dma((n,)), dma((n,)), dma((n,)), dma((n,)),
             dma((nh,)), dma((nh,)), dma((n,)), dma((n,)),
-            dma((n,)), dma((n,)), dma, dma,
+            dma((2, n)), dma((2, n)), dma, dma,
         ],
         compiler_params=pltpu.CompilerParams(
             collective_id=0, has_side_effects=True, vmem_limit_bytes=56 * 2**20
         ),
     )(
         flat(query), flat(key), flat(value), flat(lin_query), flat(lin_key), gain,
-        flat(cotangent), key_block, key_block,
+        flat(cotangent), key_block.T, key_block.T,
     )
-    return tuple(x.reshape(heads, rows, width) for x in outs[:6]) + (outs[6],)
+    return tuple(
+        pl.pallas_call(
+            hand_out,
+            out_shape=[jax.ShapeDtypeStruct((heads, rows, width), bf16)] * 6 + [total],
+            in_specs=[hbm] * 2,
+            out_specs=[hbm] * 7,
+            scratch_shapes=[dma((7,))],
+        )(stacked, gains)
+    )
 
 
 def solution(mesh):

time: 70.3 us -> 80.1 us (1.14)
  the two profiles are of different devices: /device:TPU:11 before, /device:TPU:0 now
where the time goes in v2:
time: 80.1 us; the launch traced here: 80 us
  Pallas kernels  79.3 us (99%)
    pallas_call x1, Pallas kernels, per_device(): pl.pallas_call(functools.partial(kernel, n, nh, width ** (-0.5)), out_sha...  54.3 us
    pallas_call x1, Pallas kernels, per_device(): pl.pallas_call(hand_out, out_shape=[jax.ShapeDtypeStruct((heads, rows, wi...  25 us

profile of v2, /device:TPU:0, one launch (start us, length us, event | category | flops | bytes accessed | tf_op | source)
XLA Modules:
  0.0 80.0 jit_solution(14001802265404100280)
XLA Ops:
  0.6 54.3 %shard_map.135 = (bf16[6,512,128]{2,1,0:T(8,128)(2,1)}, f32[1,128]{1,0:T(1,128)}) custom-call(bf16[512,128]{1,0:T(8,128)(2,1)} %bitcast.7, bf16[512,128]{1,0:T(8,128)(2,1)} %bitcast.8, bf16[512,128]{1,0:T(8,128)(2,1)} %bitcast.9, bf16[512,128]{1,0:T(8,128)(2,1)} %bitcast.10, bf16[512,128]{1,0:T(8,128)(2,1)} %bitcast.11, f32[1,128]{1,0:T(1,128)} %gain.1, ...), custom_call_target="tpu_custom_call" | custom-call | tf_op jit(solution)/shard_map/pallas_call | solution.py:388
  55.0 25.0 %shard_map.136 = (bf16[1,512,128]{2,1,0:T(8,128)(2,1)}, bf16[1,512,128]{2,1,0:T(8,128)(2,1)}, bf16[1,512,128]{2,1,0:T(8,128)(2,1)}, bf16[1,512,128]{2,1,0:T(8,12...) custom-call(bf16[6,512,128]{2,1,0:T(8,128)(2,1)} %get-tuple-element.9.stacked, ...), custom_call_target="tpu_custom_call" | custom-call | tf_op jit(solution)/shard_map/pallas_call | solution.py:428

commit v3 on v2

--- a/solution.py
+++ b/solution.py
@@ -51,7 +51,7 @@
     out, gg,
     kvsend, kvbuf, kvext, stsend, stbuf, grsend, grbuf, hsend, hbuf, ggsend, ggbuf,
     gfsend, gfbuf, gbsend, gbbuf, att, wn, wf, dsf, pbf, mix,
-    kv_s, kv_r, pv_s, pv_r, st_s, st_r, gr_s, gr_r, h_s, h_r, gg_s, gg_r, gf_s, gf_r, gb_s, gb_r,
+    kv_s, kv_r, pv_s, pv_r, st_s, st_r, gr_s, gr_r, h_s, h_r, gg_s, gg_r, gf_s, gf_r, gb_s, gb_r, fw_s,
 ):
     rows, width = q.shape
     blk = BLK
@@ -110,8 +110,38 @@
     def _():
         prev_copy(me + 1).start()
 
-    loop(0, n - 1 - me, lambda i: kv_copy(0, me, n - 1 - i).start())
-    loop(0, n - 1 - me, lambda i: kv_copy(1, me, n - 1 - i).start())
+    odd = me % 2
+    pair = me // 2
+    ahead = n // 2 - 1 - pair
+    partner = me + 1 - 2 * odd
+
+    def kv_pass(side, s):
+        return link(
+            kvbuf.at[side, s], kvbuf.at[side, s], fw_s.at[side, s], kv_r.at[side, s],
+            "seq", partner,
+        )
+
+    def kv_take(side):
+        def take_and_pass(i):
+            s = me - 2 - 2 * i
+            kv_copy(side, s, s).wait_recv()
+            kv_pass(side, s).start()
+
+        loop(0, pair, take_and_pass)
+
+    def kv_rest(side):
+        def take(i):
+            s = 1 - odd + 2 * i
+            kv_copy(side, s, s).wait_recv()
+
+        loop(0, pair + odd, take)
+
+    for side in range(2):
+        loop(0, ahead, lambda i: kv_copy(side, me, me + 2 * (ahead - i)).start())
+
+        @pl.when(odd == 0)
+        def _():
+            kv_copy(side, me, me + 1).start()
 
     @pl.when(me == 0)
     def _():
@@ -147,9 +177,11 @@
         prev_copy(me - 1).wait_recv()
 
     near_scores(0)
-    loop(0, me, lambda s: kv_copy(0, s, s).wait_recv())
+    kv_take(0)
+    kv_rest(0)
     kfar = kvbuf[0].reshape(n * blk, width)
     first = lax.broadcasted_iota(jnp.int32, (1, n * blk), 1) // blk * per_dev
+    kv_take(1)
     inv_total = []
     near_sum = []
     for g in range(per_dev):
@@ -175,7 +207,7 @@
         wf[at, :] = ef
         pbf[at, :] = ef.astype(bf16)
 
-    loop(0, me, lambda s: kv_copy(1, s, s).wait_recv())
+    kv_rest(1)
     vfar = kvbuf[1].reshape(n * blk, width)
     far_sum = dot(pbf[...], vfar, 1, 0)
     for g in range(per_dev):
@@ -346,8 +378,6 @@
         gb_copy(me - 1).wait_send()
 
     def sent_up(d):
-        kv_copy(0, me, d).wait_send()
-        kv_copy(1, me, d).wait_send()
         st_copy(me, d).wait_send()
         gg_copy(me, d).wait_send()
 
@@ -358,6 +388,14 @@
         gg_copy(me, d).wait_send()
 
     loop(me + 1, n, sent_up)
+    for side in range(2):
+        loop(0, ahead, lambda i: kv_copy(side, me, me + 2 * (ahead - i)).wait_send())
+        loop(0, pair, lambda i: kv_pass(side, me - 2 - 2 * i).wait_send())
+
+        @pl.when(odd == 0)
+        def _():
+            kv_copy(side, me, me + 1).wait_send()
+
     loop(0, me, sent_down)
     loop(0, hd, lambda d: h_copy(hd, d).wait_send())
     loop(hd + 1, nh, lambda d: h_copy(hd, d).wait_send())
@@ -415,7 +453,7 @@
             dma((2, n)), dma((2, n)), dma, dma,
             dma((n,)), dma((n,)), dma((n,)), dma((n,)),
             dma((nh,)), dma((nh,)), dma((n,)), dma((n,)),
-            dma((2, n)), dma((2, n)), dma, dma,
+            dma((2, n)), dma((2, n)), dma, dma, dma((2, n)),
         ],
         compiler_params=pltpu.CompilerParams(
             collective_id=0, has_side_effects=True, vmem_limit_bytes=56 * 2**20
@@ -429,7 +467,7 @@
             hand_out,
             out_shape=[jax.ShapeDtypeStruct((heads, rows, width), bf16)] * 6 + [total],
             in_specs=[hbm] * 2,
-            out_specs=[hbm] * 7,
+            out_specs=[vm] * 7,
             scratch_shapes=[dma((7,))],
         )(stacked, gains)
     )

time: 80.1 us -> 53.3 us (0.67)
  Pallas kernels: 79.3 us -> 52.2 us
    pallas_call x1, Pallas kernels: 25 us -> 2.14 us  [per_device(): pl.pallas_call(hand_out, out_shape=[jax.ShapeDtypeStruct((heads, rows, wi...]
    pallas_call x1, Pallas kernels: 54.3 us -> 50.1 us  [per_device(): pl.pallas_call(functools.partial(kernel, n, nh, width ** (-0.5)), out_sha...]
where the time goes in v3:
time: 53.3 us; the launch traced here: 52.8 us
  Pallas kernels  52.2 us (98%)
  between operations  0.64 us (1%)
    pallas_call x1, Pallas kernels, per_device(): pl.pallas_call(functools.partial(kernel, n, nh, width ** (-0.5)), out_sha...  50.1 us
    pallas_call x1, Pallas kernels, per_device(): pl.pallas_call(hand_out, out_shape=[jax.ShapeDtypeStruct((heads, rows, wi...  2.14 us

profile of v3, /device:TPU:0, one launch (start us, length us, event | category | flops | bytes accessed | tf_op | source)
XLA Modules:
  0.0 52.8 jit_solution(3983756400891047599)
XLA Ops:
  0.6 50.1 %shard_map.135 = (bf16[6,512,128]{2,1,0:T(8,128)(2,1)}, f32[1,128]{1,0:T(1,128)}) custom-call(bf16[512,128]{1,0:T(8,128)(2,1)} %bitcast.7, bf16[512,128]{1,0:T(8,128)(2,1)} %bitcast.8, bf16[512,128]{1,0:T(8,128)(2,1)} %bitcast.9, bf16[512,128]{1,0:T(8,128)(2,1)} %bitcast.10, bf16[512,128]{1,0:T(8,128)(2,1)} %bitcast.11, f32[1,128]{1,0:T(1,128)} %gain.1, ...), custom_call_target="tpu_custom_call" | custom-call | tf_op jit(solution)/shard_map/pallas_call | solution.py:426
  50.7 2.1 %shard_map.136 = (bf16[1,512,128]{2,1,0:T(8,128)(2,1)}, bf16[1,512,128]{2,1,0:T(8,128)(2,1)}, bf16[1,512,128]{2,1,0:T(8,128)(2,1)}, bf16[1,512,128]{2,1,0:T(8,12...) custom-call(bf16[6,512,128]{2,1,0:T(8,128)(2,1)} %get-tuple-element.9.stacked, ...), custom_call_target="tpu_custom_call" | custom-call | tf_op jit(solution)/shard_map/pallas_call | solution.py:466
